TPU v7x, 256 devices: a whole 4x4x8 slice. The times are simulated.
256 devices in a mesh: dp: 32 (over y, z), cent: 8 (over x, core).
Axes of the slice: x: 4, y: 4, z: 8, core: 2. Of those that a mesh axis runs over, the one named last changes fastest.
Arguments:
- stream: bfloat16 [65536, 768], P('dp'), may hold values from -6 to 6
- sample_index: int32 [32768], P('dp'), may hold values from 0 to 2047
- centroids: float32 [16384, 768], P(('cent', 'dp')), may hold values from -6 to 6
- first_moment: float32 [16384, 768], P(('cent', 'dp')), may hold values from -3 to 3
- second_moment: float32 [16384, 768], P(('cent', 'dp')), may hold values from 0.01 to 1
Outputs:
- new_centroids: float32 [16384, 768], P(('cent', 'dp'))
- new_first: float32 [16384, 768], P(('cent', 'dp'))
- new_second: float32 [16384, 768], P(('cent', 'dp'))
All inputs are finite; a program needn't handle non-finite values.
Results may differ from a plain program's by a relative error of at most 0.0003.
Values may be sent and summed in bfloat16 or wider, within the bound.
A program may use at most 64 MiB of HBM per device.

v0:
```python
import math
import jax
import jax.numpy as jnp
from jax import lax
from jax.sharding import PartitionSpec as P

KB = 16384
ITERS = 3
temper = 2.0
beta_one = 0.9
beta_two = 0.99
step_rate = 0.05
epsilon = 1e-08


def per_device(stream, sample_index, centroids, first_moment, second_moment):
    embedded = stream[sample_index]
    local_rows = embedded.shape[0]
    total_rows = local_rows * lax.axis_size("dp")
    balance = math.log(total_rows / KB)
    rounded = centroids.astype(jnp.bfloat16)
    shard_piece = lax.all_gather(rounded, "dp", axis=0, tiled=True)
    squares = jnp.sum(shard_piece.astype(jnp.float32) ** 2, axis=1)
    product = lax.dot_general(
        embedded, shard_piece, (((1,), (1,)), ((), ())), preferred_element_type=jnp.float32
    )
    logits = (2.0 * product - squares[None, :]) / temper

    def row_potential(column_pot):
        shifted = logits + column_pot[None, :]
        highest = jnp.max(shifted, axis=1)
        summed = jnp.sum(jnp.exp(shifted - highest[:, None]), axis=1)
        overall = lax.pmax(highest, "cent")
        summed = lax.psum(summed * jnp.exp(highest - overall), "cent")
        highest = overall
        return -(highest + jnp.log(summed))

    column_pot = jnp.zeros((logits.shape[1],), jnp.float32)
    for sweep_index in range(ITERS):
        column_shifted = logits + row_potential(column_pot)[:, None]
        column_highest = jnp.max(column_shifted, axis=0)
        column_summed = jnp.sum(jnp.exp(column_shifted - column_highest[None, :]), axis=0)
        column_overall = lax.pmax(column_highest, "dp")
        column_summed = lax.psum(column_summed * jnp.exp(column_highest - column_overall), "dp")
        column_highest = column_overall
        column_pot = balance - (column_highest + jnp.log(column_summed))
    row_pot = row_potential(column_pot)
    transport = jnp.exp(logits + row_pot[:, None] + column_pot[None, :]).astype(jnp.bfloat16)
    weighted = lax.dot_general(
        transport, embedded, (((0,), (0,)), ((), ())), preferred_element_type=jnp.float32
    )
    weight_mass = jnp.sum(transport.astype(jnp.float32), axis=0)
    weighted, weight_mass = lax.psum((weighted, weight_mass), "dp")
    owned_rows = centroids.shape[0]
    offset_rows = lax.axis_index("dp") * owned_rows
    weighted = lax.dynamic_slice_in_dim(weighted, offset_rows, owned_rows, 0)
    weight_mass = lax.dynamic_slice_in_dim(weight_mass, offset_rows, owned_rows, 0)
    gradient = (weight_mass[:, None] * centroids - weighted) * (KB / total_rows)
    new_first = beta_one * first_moment + (1.0 - beta_one) * gradient
    new_second = beta_two * second_moment + (1.0 - beta_two) * gradient * gradient
    new_centroids = centroids - step_rate * new_first / (jnp.sqrt(new_second) + epsilon)
    return (new_centroids, new_first, new_second)


def solution(mesh):
    return jax.shard_map(
        per_device,
        mesh=mesh,
        in_specs=(
            P("dp", None),
            P("dp"),
            P(("cent", "dp"), None),
            P(("cent", "dp"), None),
            P(("cent", "dp"), None),
        ),
        out_specs=(P(("cent", "dp"), None), P(("cent", "dp"), None), P(("cent", "dp"), None)),
        check_vma=False,
    )
```

profile of v0, /device:TPU:1, one launch (start us, length us, event | category | flops | bytes accessed | tf_op | source)
XLA Modules:
  0.0 889.1 jit_solution(12046903474257052355)
XLA Ops:
  9.7 5.2 gather_fusion
  15.0 76.0 %all-gather.2.cloned.1.call-done = bf16[2048,768]{1,0:T(8,128)(2,1)} async-done(((bf16[64,768]{1,0:T(8,128)(2,1)}), bf16[2048,768]{1,0:T(8,128)(2,1)}) %all-gather.2.cloned.1.call-update) | async-done | bytes 3145744 | tf_op jit(solution)/shard_map/all_gather | solution.py:22
  93.6 9.1 %fusion.2 = (f32[1024]{0:T(1024)S(1)}, f32[1024,2048]{1,0:T(8,128)}) fusion(f32[2048]{0:T(1024)S(1)} %multiply_reduce_fusion, bf16[1024,768]{1,0:T(8,128)(2,1)} %gather_fusion, bf16[2048,768]{1,0:T(8,128)(2,1)} %all-gather.2.cloned.1.call-done), kind=kOutput, calls=%fused_computation.39 | convolution fusion | flops 3229613056 | bytes 13119488 | tf_op jit(solution)/shard_map/dot_general | solution.py:24
  102.6 16.4 %pmax.49 = f32[1024]{0:T(1024)S(1)} all-reduce(f32[1024]{0:T(1024)S(1)} %get-tuple-element.6), channel_id=1, replica_groups=mesh['dp'=32,'cent'=8] {'cent'}, use_global_device_ids=true, to_apply=%region_2.0 | all-reduce | flops 1024 | bytes 8192 | tf_op jit(solution)/shard_map/pmax | solution.py:33
  119.0 4.6 exponential_reduce_fusion.6
  123.6 12.4 %psum.63 = f32[1024]{0:T(1024)S(1)} all-reduce(f32[1024]{0:T(1024)S(1)} %exponential_multiply_fusion.6), channel_id=1, replica_groups=mesh['dp'=32,'cent'=8] {'cent'}, use_global_device_ids=true, to_apply=%region_4.0 | all-reduce | flops 1024 | bytes 8192 | tf_op jit(solution)/shard_map/psum | solution.py:34
  140.1 4.3 exponential_reduce_fusion.5
  144.4 58.9 %pmax.50 = f32[2048]{0:T(1024)S(1)} all-reduce(f32[2048]{0:T(1024)S(1)} %add_reduce_fusion.5), channel_id=1, replica_groups=mesh['dp'=32,'cent'=8] {'dp'}, use_global_device_ids=true, to_apply=%region_6.0 | all-reduce | flops 2048 | bytes 16384 | tf_op jit(solution)/shard_map/pmax | solution.py:43
  203.3 56.7 %psum.64 = f32[2048]{0:T(1024)S(1)} all-reduce(f32[2048]{0:T(1024)S(1)} %exponential_multiply_fusion.2), channel_id=1, replica_groups=mesh['dp'=32,'cent'=8] {'dp'}, use_global_device_ids=true, to_apply=%region_8.0 | all-reduce | flops 2048 | bytes 16384 | tf_op jit(solution)/shard_map/psum | solution.py:44
  260.1 4.0 add_reduce_fusion.4
  264.1 4.4 exponential_reduce_fusion.4
  268.5 40.3 %pmax.51 = f32[1024]{0:T(1024)S(1)} all-reduce(f32[1024]{0:T(1024)S(1)} %add_reduce_fusion.4), channel_id=1, replica_groups=mesh['dp'=32,'cent'=8] {'cent'}, use_global_device_ids=true, to_apply=%region_10.0 | all-reduce | flops 1024 | bytes 8192 | tf_op jit(solution)/shard_map/pmax | solution.py:33
  308.8 12.4 %psum.65 = f32[1024]{0:T(1024)S(1)} all-reduce(f32[1024]{0:T(1024)S(1)} %exponential_multiply_fusion.5), channel_id=1, replica_groups=mesh['dp'=32,'cent'=8] {'cent'}, use_global_device_ids=true, to_apply=%region_12.0 | all-reduce | flops 1024 | bytes 8192 | tf_op jit(solution)/shard_map/psum | solution.py:34
  321.2 4.0 add_reduce_fusion.3
  325.3 4.3 exponential_reduce_fusion.3
  329.6 59.1 %pmax.52 = f32[2048]{0:T(1024)S(1)} all-reduce(f32[2048]{0:T(1024)S(1)} %add_reduce_fusion.3), channel_id=1, replica_groups=mesh['dp'=32,'cent'=8] {'dp'}, use_global_device_ids=true, to_apply=%region_14.0 | all-reduce | flops 2048 | bytes 16384 | tf_op jit(solution)/shard_map/pmax | solution.py:43
  388.7 57.2 %psum.66 = f32[2048]{0:T(1024)S(1)} all-reduce(f32[2048]{0:T(1024)S(1)} %exponential_multiply_fusion.1), channel_id=1, replica_groups=mesh['dp'=32,'cent'=8] {'dp'}, use_global_device_ids=true, to_apply=%region_16.0 | all-reduce | flops 2048 | bytes 16384 | tf_op jit(solution)/shard_map/psum | solution.py:44
  446.0 4.0 add_reduce_fusion.2
  450.0 4.4 exponential_reduce_fusion.2
  454.4 39.6 %pmax.53 = f32[1024]{0:T(1024)S(1)} all-reduce(f32[1024]{0:T(1024)S(1)} %add_reduce_fusion.2), channel_id=1, replica_groups=mesh['dp'=32,'cent'=8] {'cent'}, use_global_device_ids=true, to_apply=%region_18.0 | all-reduce | flops 1024 | bytes 8192 | tf_op jit(solution)/shard_map/pmax | solution.py:33
  494.0 12.4 %psum.67 = f32[1024]{0:T(1024)S(1)} all-reduce(f32[1024]{0:T(1024)S(1)} %exponential_multiply_fusion.4), channel_id=1, replica_groups=mesh['dp'=32,'cent'=8] {'cent'}, use_global_device_ids=true, to_apply=%region_20.0 | all-reduce | flops 1024 | bytes 8192 | tf_op jit(solution)/shard_map/psum | solution.py:34
  506.4 4.0 add_reduce_fusion.1
  510.4 4.3 exponential_reduce_fusion.1
  514.7 59.2 %pmax.54 = f32[2048]{0:T(1024)S(1)} all-reduce(f32[2048]{0:T(1024)S(1)} %add_reduce_fusion.1), channel_id=1, replica_groups=mesh['dp'=32,'cent'=8] {'dp'}, use_global_device_ids=true, to_apply=%region_22.0 | all-reduce | flops 2048 | bytes 16384 | tf_op jit(solution)/shard_map/pmax | solution.py:43
  573.9 57.0 %psum.68 = f32[2048]{0:T(1024)S(1)} all-reduce(f32[2048]{0:T(1024)S(1)} %exponential_multiply_fusion), channel_id=1, replica_groups=mesh['dp'=32,'cent'=8] {'dp'}, use_global_device_ids=true, to_apply=%region_24.0 | all-reduce | flops 2048 | bytes 16384 | tf_op jit(solution)/shard_map/psum | solution.py:44
  635.0 4.4 exponential_reduce_fusion
  639.4 39.6 %pmax.55 = f32[1024]{0:T(1024)S(1)} all-reduce(f32[1024]{0:T(1024)S(1)} %add_reduce_fusion), channel_id=1, replica_groups=mesh['dp'=32,'cent'=8] {'cent'}, use_global_device_ids=true, to_apply=%region_26.0 | all-reduce | flops 1024 | bytes 8192 | tf_op jit(solution)/shard_map/pmax | solution.py:33
  679.0 12.4 %psum.69 = f32[1024]{0:T(1024)S(1)} all-reduce(f32[1024]{0:T(1024)S(1)} %exponential_multiply_fusion.3), channel_id=1, replica_groups=mesh['dp'=32,'cent'=8] {'cent'}, use_global_device_ids=true, to_apply=%region_28.0 | all-reduce | flops 1024 | bytes 8192 | tf_op jit(solution)/shard_map/psum | solution.py:34
  692.0 10.4 %fusion.1 = f32[2048,768]{1,0:T(8,128)} fusion(bf16[1024,768]{1,0:T(8,128)(2,1)} %gather_fusion, f32[1024,2048]{1,0:T(8,128)} %get-tuple-element.7, f32[1024]{0:T(1024)S(1)} %add_negate_fusion, f32[2048]{0:T(1024)S(1)} %add_subtract_fusion), kind=kOutput, calls=%fused_computation.38 | convolution fusion | flops 3227516928 | bytes 16265216 | tf_op jit(solution)/shard_map/dot_general | solution.py:49
  702.4 4.3 convert_reduce_fusion
  706.8 61.3 %psum.70 = f32[2048]{0:T(1024)S(1)} all-reduce(f32[2048]{0:T(1024)S(1)} %convert_reduce_fusion), channel_id=1, replica_groups=mesh['dp'=32,'cent'=8] {'dp'}, use_global_device_ids=true, to_apply=%region_30.0 | all-reduce | flops 2048 | bytes 16384 | tf_op jit(solution)/shard_map/psum | solution.py:53
  768.1 112.1 %all-reduce.2.cloned.1.call-done = f32[2048,768]{1,0:T(8,128)} async-done(((f32[2048,768]{1,0:T(8,128)}), f32[2048,768]{1,0:T(8,128)}) %all-reduce.2.cloned.1.call-update) | async-done | bytes 6291472 | tf_op jit(solution)/shard_map/psum | solution.py:53
  (33 shorter events, 15.9 us)
Async XLA Ops:
  7.2 2.6 copy-start
  7.2 83.8 %all-gather.2.cloned.1.call-start = ((), (), s32[]{:S(2)}) async-start(), calls=%async_computation | async-start | bytes 3244032 | tf_op jit(solution)/shard_map/all_gather | solution.py:22
  9.0 871.3 %all-reduce.2.cloned.1.call-start = ((), (), s32[]{:S(2)}) async-start(), calls=%async_computation.1 | async-start | bytes 12582912 | tf_op jit(solution)/shard_map/psum | solution.py:53
  691.4 0.6 copy-start.3
  702.4 177.9 %copy-start.1 = (f32[64,768]{1,0:T(8,128)S(1)}, f32[64,768]{1,0:T(8,128)}, u32[]{:S(2)}) copy-start(f32[64,768]{1,0:T(8,128)} %param.7) | copy-start | bytes 589828
  702.4 177.9 %copy-start.2 = (f32[64,768]{1,0:T(8,128)S(1)}, f32[64,768]{1,0:T(8,128)}, u32[]{:S(2)}) copy-start(f32[64,768]{1,0:T(8,128)} %param.8) | copy-start | bytes 589828
Sparse Core Ops, SparseCore 0:
  11.2 79.7 all-gather.1
  702.5 177.6 all-reduce.1
where the time goes:
time: 890 us; the launch traced here: 889 us
  blocking collectives  595 us (67%)
  waiting for transfers between devices  188 us (21%)
  other arithmetic  66.1 us (7%)
  matrix products  19.4 us (2%)
  between operations  14.3 us (2%)
    pmax x3, blocking collectives, per_device(): column_overall = lax.pmax(column_highest, 'dp')  177 us
    psum x3, blocking collectives, per_device(): lax.psum(column_summed * jnp.exp(column_highest - column_overall), 'dp')  171 us
    pmax x4, blocking collectives, row_potential(): overall = lax.pmax(highest, 'cent')  136 us
    psum x1, waiting for transfers between devices, per_device(): weighted, weight_mass = lax.psum((weighted, weight_mass), 'dp')  112 us
    all_gather x1, waiting for transfers between devices, per_device(): shard_piece = lax.all_gather(rounded, 'dp', axis=0, tiled=True)  76 us
    psum x1, blocking collectives, per_device(): weighted, weight_mass = lax.psum((weighted, weight_mass), 'dp')  61.3 us
    psum x4, blocking collectives, row_potential(): summed = lax.psum(summed * jnp.exp(highest - overall), 'cent')  49.7 us
  transfers between devices with their start and end apart: 2, of which 2 were waited for; matrix products, arithmetic and copies ran while one was open for 1% of the time, Pallas kernels for 0%

commit v1 on v0

--- a/solution.py
+++ b/solution.py
@@ -19,7 +19,9 @@
     total_rows = local_rows * lax.axis_size("dp")
     balance = math.log(total_rows / KB)
     rounded = centroids.astype(jnp.bfloat16)
-    shard_piece = lax.all_gather(rounded, "dp", axis=0, tiled=True)
+    shard_piece = jnp.concatenate(
+        lax.all_to_all(jnp.stack([rounded] * lax.axis_size("dp")), "dp", 0, 0), axis=0
+    )
     squares = jnp.sum(shard_piece.astype(jnp.float32) ** 2, axis=1)
     product = lax.dot_general(
         embedded, shard_piece, (((1,), (1,)), ((), ())), preferred_element_type=jnp.float32

time: 890 us -> 893 us (level)
  starting transfers between devices: 0.08 us -> 12.2 us
  waiting for transfers between devices: 188 us -> 178 us
    all_gather x1 -> x0, waiting for transfers between devices: 76 us -> none  [per_device(): shard_piece = lax.all_gather(rounded, 'dp', axis=0, tiled=True)]
    all_to_all x0 -> x1, waiting for transfers between devices: none -> 66.2 us  [per_device(): lax.all_to_all(jnp.stack([rounded] * lax.axis_size('dp')), 'dp', 0, 0)]
    all_to_all x0 -> x1, starting transfers between devices: none -> 12.1 us  [per_device(): lax.all_to_all(jnp.stack([rounded] * lax.axis_size('dp')), 'dp', 0, 0)]
where the time goes in v1:
time: 893 us; the launch traced here: 892 us
  blocking collectives  595 us (67%)
  waiting for transfers between devices  178 us (20%)
  other arithmetic  64.8 us (7%)
  matrix products  19.4 us (2%)
  between operations  14.3 us (2%)
  starting transfers between devices  12.2 us (1%)
    pmax x3, blocking collectives, per_device(): column_overall = lax.pmax(column_highest, 'dp')  177 us
    psum x3, blocking collectives, per_device(): lax.psum(column_summed * jnp.exp(column_highest - column_overall), 'dp')  171 us
    pmax x4, blocking collectives, row_potential(): overall = lax.pmax(highest, 'cent')  136 us
    psum x1, waiting for transfers between devices, per_device(): weighted, weight_mass = lax.psum((weighted, weight_mass), 'dp')  112 us
    all_to_all x1, waiting for transfers between devices, per_device(): lax.all_to_all(jnp.stack([rounded] * lax.axis_size('dp')), 'dp', 0, 0)  66.2 us
    psum x1, blocking collectives, per_device(): weighted, weight_mass = lax.psum((weighted, weight_mass), 'dp')  61.2 us
    psum x4, blocking collectives, row_potential(): summed = lax.psum(summed * jnp.exp(highest - overall), 'cent')  49.7 us
  transfers between devices with their start and end apart: 2, of which 2 were waited for; matrix products, arithmetic and copies ran while one was open for 1% of the time, Pallas kernels for 0%

profile of v1, /device:TPU:1, one launch (start us, length us, event | category | flops | bytes accessed | tf_op | source)
XLA Modules:
  0.0 892.0 jit_solution(1177248562189263842)
XLA Ops:
  10.3 12.1 %all-to-all-start = ((bf16[32,64,768]{2,1,0:T(8,128)(2,1)}), bf16[32,64,768]{2,1,0:T(8,128)(2,1)}, u32[]{:S(2)}, u32[]{:S(2)}) async-start(bf16[32,64,768]{2,1,0:T(8,128)(2,1)} %stack.2), calls=%async_computation | async-start | bytes 6291456 | tf_op jit(solution)/shard_map/all_to_all | solution.py:23
  22.6 5.2 gather_fusion
  27.8 66.2 %all-to-all-done = bf16[32,64,768]{2,1,0:T(8,128)(2,1)} async-done(((bf16[32,64,768]{2,1,0:T(8,128)(2,1)}), bf16[32,64,768]{2,1,0:T(8,128)(2,1)}, u32[]{:S(2)}, u32[]{:S(2)}) %all-to-all-start) | async-done | bytes 3145760 | tf_op jit(solution)/shard_map/all_to_all | solution.py:23
  96.6 9.1 %fusion.2 = (f32[1024]{0:T(1024)S(1)}, f32[1024,2048]{1,0:T(8,128)}) fusion(f32[2048]{0:T(1024)S(1)} %sub.102, bf16[1024,768]{1,0:T(8,128)(2,1)} %gather_fusion, bf16[2048,768]{1,0:T(8,128)(2,1)} %bitcast), kind=kOutput, calls=%fused_computation.39 | convolution fusion | flops 3229613056 | bytes 13119488 | tf_op jit(solution)/shard_map/dot_general | solution.py:26
  105.7 15.9 %pmax.49 = f32[1024]{0:T(1024)S(1)} all-reduce(f32[1024]{0:T(1024)S(1)} %get-tuple-element.6), channel_id=1, replica_groups=mesh['dp'=32,'cent'=8] {'cent'}, use_global_device_ids=true, to_apply=%region_2.0 | all-reduce | flops 1024 | bytes 8192 | tf_op jit(solution)/shard_map/pmax | solution.py:35
  121.5 4.6 exponential_reduce_fusion.6
  126.2 12.4 %psum.63 = f32[1024]{0:T(1024)S(1)} all-reduce(f32[1024]{0:T(1024)S(1)} %exponential_multiply_fusion.6), channel_id=1, replica_groups=mesh['dp'=32,'cent'=8] {'cent'}, use_global_device_ids=true, to_apply=%region_4.0 | all-reduce | flops 1024 | bytes 8192 | tf_op jit(solution)/shard_map/psum | solution.py:36
  138.6 4.0 add_reduce_fusion.5
  142.6 4.3 exponential_reduce_fusion.5
  146.9 59.0 %pmax.50 = f32[2048]{0:T(1024)S(1)} all-reduce(f32[2048]{0:T(1024)S(1)} %add_reduce_fusion.5), channel_id=1, replica_groups=mesh['dp'=32,'cent'=8] {'dp'}, use_global_device_ids=true, to_apply=%region_6.0 | all-reduce | flops 2048 | bytes 16384 | tf_op jit(solution)/shard_map/pmax | solution.py:45
  206.0 56.8 %psum.64 = f32[2048]{0:T(1024)S(1)} all-reduce(f32[2048]{0:T(1024)S(1)} %exponential_multiply_fusion.2), channel_id=1, replica_groups=mesh['dp'=32,'cent'=8] {'dp'}, use_global_device_ids=true, to_apply=%region_8.0 | all-reduce | flops 2048 | bytes 16384 | tf_op jit(solution)/shard_map/psum | solution.py:46
  262.8 4.0 add_reduce_fusion.4
  266.8 4.4 exponential_reduce_fusion.4
  271.2 40.5 %pmax.51 = f32[1024]{0:T(1024)S(1)} all-reduce(f32[1024]{0:T(1024)S(1)} %add_reduce_fusion.4), channel_id=1, replica_groups=mesh['dp'=32,'cent'=8] {'cent'}, use_global_device_ids=true, to_apply=%region_10.0 | all-reduce | flops 1024 | bytes 8192 | tf_op jit(solution)/shard_map/pmax | solution.py:35
  311.7 12.4 %psum.65 = f32[1024]{0:T(1024)S(1)} all-reduce(f32[1024]{0:T(1024)S(1)} %exponential_multiply_fusion.5), channel_id=1, replica_groups=mesh['dp'=32,'cent'=8] {'cent'}, use_global_device_ids=true, to_apply=%region_12.0 | all-reduce | flops 1024 | bytes 8192 | tf_op jit(solution)/shard_map/psum | solution.py:36
  328.1 4.3 exponential_reduce_fusion.3
  332.4 59.1 %pmax.52 = f32[2048]{0:T(1024)S(1)} all-reduce(f32[2048]{0:T(1024)S(1)} %add_reduce_fusion.3), channel_id=1, replica_groups=mesh['dp'=32,'cent'=8] {'dp'}, use_global_device_ids=true, to_apply=%region_14.0 | all-reduce | flops 2048 | bytes 16384 | tf_op jit(solution)/shard_map/pmax | solution.py:45
  391.6 57.2 %psum.66 = f32[2048]{0:T(1024)S(1)} all-reduce(f32[2048]{0:T(1024)S(1)} %exponential_multiply_fusion.1), channel_id=1, replica_groups=mesh['dp'=32,'cent'=8] {'dp'}, use_global_device_ids=true, to_apply=%region_16.0 | all-reduce | flops 2048 | bytes 16384 | tf_op jit(solution)/shard_map/psum | solution.py:46
  448.9 4.0 add_reduce_fusion.2
  452.9 4.4 exponential_reduce_fusion.2
  457.3 39.6 %pmax.53 = f32[1024]{0:T(1024)S(1)} all-reduce(f32[1024]{0:T(1024)S(1)} %add_reduce_fusion.2), channel_id=1, replica_groups=mesh['dp'=32,'cent'=8] {'cent'}, use_global_device_ids=true, to_apply=%region_18.0 | all-reduce | flops 1024 | bytes 8192 | tf_op jit(solution)/shard_map/pmax | solution.py:35
  496.9 12.4 %psum.67 = f32[1024]{0:T(1024)S(1)} all-reduce(f32[1024]{0:T(1024)S(1)} %exponential_multiply_fusion.4), channel_id=1, replica_groups=mesh['dp'=32,'cent'=8] {'cent'}, use_global_device_ids=true, to_apply=%region_20.0 | all-reduce | flops 1024 | bytes 8192 | tf_op jit(solution)/shard_map/psum | solution.py:36
  513.3 4.3 exponential_reduce_fusion.1
  517.6 59.2 %pmax.54 = f32[2048]{0:T(1024)S(1)} all-reduce(f32[2048]{0:T(1024)S(1)} %add_reduce_fusion.1), channel_id=1, replica_groups=mesh['dp'=32,'cent'=8] {'dp'}, use_global_device_ids=true, to_apply=%region_22.0 | all-reduce | flops 2048 | bytes 16384 | tf_op jit(solution)/shard_map/pmax | solution.py:45
  576.8 57.0 %psum.68 = f32[2048]{0:T(1024)S(1)} all-reduce(f32[2048]{0:T(1024)S(1)} %exponential_multiply_fusion), channel_id=1, replica_groups=mesh['dp'=32,'cent'=8] {'dp'}, use_global_device_ids=true, to_apply=%region_24.0 | all-reduce | flops 2048 | bytes 16384 | tf_op jit(solution)/shard_map/psum | solution.py:46
  637.9 4.4 exponential_reduce_fusion
  642.3 39.6 %pmax.55 = f32[1024]{0:T(1024)S(1)} all-reduce(f32[1024]{0:T(1024)S(1)} %add_reduce_fusion), channel_id=1, replica_groups=mesh['dp'=32,'cent'=8] {'cent'}, use_global_device_ids=true, to_apply=%region_26.0 | all-reduce | flops 1024 | bytes 8192 | tf_op jit(solution)/shard_map/pmax | solution.py:35
  681.9 12.4 %psum.69 = f32[1024]{0:T(1024)S(1)} all-reduce(f32[1024]{0:T(1024)S(1)} %exponential_multiply_fusion.3), channel_id=1, replica_groups=mesh['dp'=32,'cent'=8] {'cent'}, use_global_device_ids=true, to_apply=%region_28.0 | all-reduce | flops 1024 | bytes 8192 | tf_op jit(solution)/shard_map/psum | solution.py:36
  694.9 10.4 %fusion.1 = f32[2048,768]{1,0:T(8,128)} fusion(bf16[1024,768]{1,0:T(8,128)(2,1)} %gather_fusion, f32[1024,2048]{1,0:T(8,128)} %get-tuple-element.7, f32[1024]{0:T(1024)S(1)} %add_negate_fusion, f32[2048]{0:T(1024)S(1)} %add_subtract_fusion), kind=kOutput, calls=%fused_computation.38 | convolution fusion | flops 3227516928 | bytes 16265216 | tf_op jit(solution)/shard_map/dot_general | solution.py:51
  705.3 4.3 convert_reduce_fusion
  709.6 61.2 %psum.70 = f32[2048]{0:T(1024)S(1)} all-reduce(f32[2048]{0:T(1024)S(1)} %convert_reduce_fusion), channel_id=1, replica_groups=mesh['dp'=32,'cent'=8] {'dp'}, use_global_device_ids=true, to_apply=%region_30.0 | all-reduce | flops 2048 | bytes 16384 | tf_op jit(solution)/shard_map/psum | solution.py:55
  770.9 112.2 %all-reduce.2.cloned.1.call-done = f32[2048,768]{1,0:T(8,128)} async-done(((f32[2048,768]{1,0:T(8,128)}), f32[2048,768]{1,0:T(8,128)}) %all-reduce.2.cloned.1.call-update) | async-done | bytes 6291472 | tf_op jit(solution)/shard_map/psum | solution.py:55
  (36 shorter events, 20.6 us)
Async XLA Ops:
  7.2 15.4 %copy-start = (bf16[2048,768]{1,0:T(8,128)(2,1)S(1)}, bf16[2048,768]{1,0:T(8,128)(2,1)}, u32[]{:S(2)}) copy-start(bf16[2048,768]{1,0:T(8,128)(2,1)} %param.5) | copy-start | bytes 9437188
  7.2 15.3 %copy-start.4 = (s32[1024]{0:T(1024)S(1)}, s32[1024]{0:T(1024)}, u32[]{:S(2)}) copy-start(s32[1024]{0:T(1024)} %param.6) | copy-start | bytes 12292
  10.3 83.7 %all-to-all-start = ((bf16[32,64,768]{2,1,0:T(8,128)(2,1)}), bf16[32,64,768]{2,1,0:T(8,128)(2,1)}, u32[]{:S(2)}, u32[]{:S(2)}) async-start(bf16[32,64,768]{2,1,0:T(8,128)(2,1)} %stack.2), calls=%async_computation | async-start | bytes 6291456 | tf_op jit(solution)/shard_map/all_to_all | solution.py:23
  22.5 860.7 %all-reduce.2.cloned.1.call-start = ((), (), s32[]{:S(2)}) async-start(), calls=%async_computation.1 | async-start | bytes 12582912 | tf_op jit(solution)/shard_map/psum | solution.py:55
  694.3 0.6 copy-start.3
  705.3 177.9 %copy-start.1 = (f32[64,768]{1,0:T(8,128)S(1)}, f32[64,768]{1,0:T(8,128)}, u32[]{:S(2)}) copy-start(f32[64,768]{1,0:T(8,128)} %param.7) | copy-start | bytes 589828
  705.3 177.9 %copy-start.2 = (f32[64,768]{1,0:T(8,128)S(1)}, f32[64,768]{1,0:T(8,128)}, u32[]{:S(2)}) copy-start(f32[64,768]{1,0:T(8,128)} %param.8) | copy-start | bytes 589828
Sparse Core Ops, SparseCore 0:
  705.4 177.7 all-reduce.1
